TPU v7x, 32 devices: a whole 2x2x4 slice. The times are simulated.
32 devices in a mesh: dp: 8 (over y, x, core), tensor: 4 (over z).
Axes of the slice: x: 2, y: 2, z: 4, core: 2. Of those that a mesh axis runs over, the one named last changes fastest.
Arguments:
- hidden: bfloat16 [1024, 8192], P('dp', 'tensor')
- rotation: float32 [8192, 8192], P('dp', 'tensor'), may hold values from -0.0625 to 0.0625
- channel_scale: float32 [8192], P('tensor')
- lengths: int32 [16], P('dp'), may hold values from 16 to 64, as said below
Outputs:
- direction: float32 [8192, 8192], P('dp', 'tensor')
- loss: float32 [], replicated
Inputs may be any that keep to these rules, and one draw needn't show every extreme that they name: `lengths`: each sequence's valid length; some sequence is full in every draw.
All inputs are finite; a program needn't handle non-finite values.
Results may differ from a plain program's by a relative error of at most 0.00075.
The roundings to bfloat16 on the way count: a program that leaves them out, or rounds other values in their place, can miss the bound.
Values may be sent and summed in bfloat16 or wider, within the bound.
A program may use at most 128 MiB of HBM per device.

v0:
```python
import math
import jax
import jax.numpy as jnp
from jax import lax
from jax.sharding import PartitionSpec as P

D = 8192
SEQ = 64


def local(hidden, rotation, channel_scale, lengths):
    narrow_rotation = rotation.astype(jnp.bfloat16)
    features = lax.all_gather(hidden, "tensor", axis=1, tiled=True)
    column_blocks = lax.all_to_all(features, "dp", split_axis=1, concat_axis=0, tiled=True)
    partial = jnp.dot(column_blocks, narrow_rotation, preferred_element_type=jnp.float32)
    rotated = lax.psum_scatter(partial, "dp", scatter_dimension=0, tiled=True)
    scaled = rotated * channel_scale[None, :]
    token_square = lax.psum(jnp.sum(scaled * scaled, axis=1), "tensor")
    step_size = 4.0 * jnp.sqrt(token_square / D + 1e-06)[:, None]
    token_index = jnp.arange(hidden.shape[0], dtype=jnp.int32)
    position = token_index % SEQ
    sequence_index = token_index // SEQ
    sequence_count = lengths.shape[0]
    owners = sequence_index[:, None] == jnp.arange(sequence_count, dtype=jnp.int32)[None, :]
    inside = position[:, None] < lengths[None, :]
    live_mask = jnp.sum(jnp.where(owners & inside, 1.0, 0.0), axis=1).astype(jnp.float32)[:, None]
    angles = math.pi * scaled / step_size
    error_local = jnp.sum(live_mask * jnp.sin(angles) ** 2)
    count_local = jnp.sum(lengths).astype(jnp.float32) / lax.axis_size("tensor")
    error_slope = (
        live_mask * (math.pi / step_size) * jnp.sin(2.0 * angles) * channel_scale[None, :]
    ).astype(jnp.bfloat16)
    gradient = lax.dot_general(
        column_blocks,
        lax.all_gather(error_slope, "dp", axis=0, tiled=True),
        (((0,), (0,)), ((), ())),
        preferred_element_type=jnp.float32,
    )
    error_sum, count = lax.psum((error_local, count_local), ("dp", "tensor"))
    grad_square = lax.psum(jnp.sum(gradient * gradient), ("dp", "tensor"))
    direction = gradient / jnp.sqrt(grad_square / (D * D) + 1e-06)
    loss = error_sum / (D * count)
    return (direction, loss)


def solution(mesh):
    return jax.shard_map(
        local,
        mesh=mesh,
        in_specs=(P("dp", "tensor"), P("dp", "tensor"), P("tensor"), P("dp")),
        out_specs=(P("dp", "tensor"), P()),
        check_vma=False,
    )
```

profile of v0, /device:TPU:0, one launch (start us, length us, event | category | flops | bytes accessed | tf_op | source)
XLA Modules:
  0.0 305.9 jit_solution(8076852472374651479)
XLA Ops:
  7.2 0.0 all-gather.3.cloned.1.call-start
  7.2 2.0 copy.11
  9.3 0.0 all-gather.3.cloned.1.call-update
  9.3 0.0 reduce-scatter.2.cloned.1.call-start
  9.3 49.5 %all-gather.3.cloned.1.call-done = bf16[128,8192]{0,1:T(8,128)(2,1)} async-done(((bf16[128,2048]{0,1:T(8,128)(2,1)}), bf16[128,8192]{0,1:T(8,128)(2,1)}) %all-gather.3.cloned.1.call-update) | async-done | bytes 2097168 | tf_op jit(solution)/shard_map/all_gather | solution.py:13
  58.8 30.2 %all_to_all.19 = bf16[128,8,1024]{0,2,1:T(8,128)(2,1)S(1)} all-to-all(bf16[128,8,1024]{0,2,1:T(8,128)(2,1)} %bitcast.11), channel_id=1, replica_groups=mesh['dp'=8,'tensor'=4] {'dp'}, dimensions={1} | all-to-all | bytes 4194304 | tf_op jit(solution)/shard_map/all_to_all | solution.py:14
  89.0 2.6 copy.12
  91.6 11.9 %fusion = f32[1024,2048]{1,0:T(8,128)} fusion(bf16[1024,1024]{1,0:T(8,128)(2,1)} %bitcast.9, f32[1024,2048]{1,0:T(8,128)} %param.5), kind=kOutput, calls=%fused_computation.2 | convolution fusion | flops 4297064448 | bytes 18874368 | tf_op jit(solution)/shard_map/dot_general | solution.py:15
  103.6 0.0 copy-start.2
  103.6 0.0 copy-start.1
  103.6 0.0 copy-start
  103.6 0.0 reduce-scatter.2.cloned.1.call-update
  103.6 0.0 all-gather.5.cloned.1.call-start
  103.6 0.6 copy-done.2
  104.2 0.1 fusion.2
  104.3 67.6 %reduce-scatter.2.cloned.1.call-done = f32[128,2048]{1,0:T(8,128)} async-done(((f32[1024,2048]{1,0:T(8,128)}), f32[128,2048]{1,0:T(8,128)}) %reduce-scatter.2.cloned.1.call-update) | async-done | bytes 1048592 | tf_op jit(solution)/shard_map/reduce_scatter | solution.py:16
  171.9 0.0 copy-done.1
  171.9 1.4 multiply_reduce_fusion.2
  173.3 11.7 %psum.28 = f32[128]{0:T(128)S(1)} all-reduce(f32[128]{0:T(128)S(1)} %multiply_reduce_fusion.2), channel_id=1, replica_groups=mesh['dp'=8,'tensor'=4] {'tensor'}, use_global_device_ids=true, to_apply=%region_3.4 | all-reduce | flops 128 | bytes 1024 | tf_op jit(solution)/shard_map/psum | solution.py:18
  185.0 9.9 %multiply_reduce_fusion.1 = (f32[]{:T(128)}, bf16[128,2048]{1,0:T(8,128)(2,1)}) fusion(f32[128]{0:T(128)S(1)} %fusion.2, f32[128]{0:T(128)S(1)} %get-tuple-element.15, f32[128,2048]{1,0:T(8,128)} %reduce-scatter.2.cloned.1.call-done, f32[2048]{0:T(1024)S(1)} %copy-done.1, f32[128]{0:T(128)S(1)} %get-tuple-element.16), kind=kLoop, calls=%fused_computation.4 | loop fusion | flops 2621439 | bytes 1582596 | tf_op jit(solution)/shard_map/reduce_sum | solution.py:28
  194.9 0.0 all-gather.5.cloned.1.call-update
  195.0 0.6 reduce_sum.49
  196.2 32.9 %all-gather.5.cloned.1.call-done = bf16[1024,2048]{1,0:T(8,128)(2,1)} async-done(((bf16[128,2048]{1,0:T(8,128)(2,1)}), bf16[1024,2048]{1,0:T(8,128)(2,1)}) %all-gather.5.cloned.1.call-update) | async-done | bytes 4194320 | tf_op jit(solution)/shard_map/all_gather | solution.py:35
  229.0 0.0 copy-done
  229.1 10.1 %multiply_reduce_fusion = (f32[]{:T(128)}, f32[2048,1024]{1,0:T(8,128)}) fusion(bf16[1024,2048]{1,0:T(8,128)(2,1)} %all-gather.5.cloned.1.call-done, bf16[1024,1024]{1,0:T(8,128)(2,1)S(1)} %bitcast.10), kind=kOutput, calls=%fused_computation.1 | convolution fusion | flops 4299161600 | bytes 14680068 | tf_op jit(solution)/shard_map/dot_general | solution.py:33
  239.2 39.6 %all-reduce = (f32[]{:T(128)}, f32[]{:T(128)}, f32[]{:T(128)}) all-reduce(f32[]{:T(128)} %get-tuple-element.17, f32[]{:T(128)} %get-tuple-element.13, f32[]{:T(128)S(6)} %div.59), channel_id=1, replica_groups=mesh['dp'=8,'tensor'=4] {'dp','tensor'}, use_global_device_ids=true, to_apply=%region_5.6 | all-reduce | flops 3 | bytes 24 | tf_op jit(solution)/shard_map/psum | solution.py:40
  279.4 8.5 %divide_bitcast_fusion = f32[1024,2048]{0,1:T(8,128)} fusion(f32[2048,1024]{1,0:T(8,128)} %get-tuple-element.18, f32[]{:T(128)S(6)} %sqrt.7), kind=kLoop, calls=%fused_computation | loop fusion | flops 2097152 | bytes 16777220 | tf_op jit(solution)/shard_map/div | solution.py:41
  287.9 9.1 %copy.13 = f32[1024,2048]{1,0:T(8,128)} copy(f32[1024,2048]{0,1:T(8,128)} %divide_bitcast_fusion) | data formatting | bytes 16777216
  (2 shorter events, 0.0 us)
Async XLA Ops:
  7.2 51.6 %all-gather.3.cloned.1.call-start = ((), (), s32[]{:S(2)}) async-start(), calls=%async_computation.2 | async-start | bytes 2621440 | tf_op jit(solution)/shard_map/all_gather | solution.py:13
  9.3 162.6 %reduce-scatter.2.cloned.1.call-start = ((), (), s32[]{:S(2)}) async-start(), calls=%async_computation.3 | async-start | bytes 9437184 | tf_op jit(solution)/shard_map/reduce_scatter | solution.py:16
  103.6 0.7 copy-start.2
  103.6 68.4 %copy-start.1 = (f32[2048]{0:T(1024)S(1)}, f32[2048]{0:T(1024)}, u32[]{:S(2)}) copy-start(f32[2048]{0:T(1024)} %param.6) | copy-start | bytes 24580
  103.6 125.5 %copy-start = (bf16[8,128,1024]{2,1,0:T(8,128)(2,1)S(1)}, bf16[8,128,1024]{2,1,0:T(8,128)(2,1)}, u32[]{:S(2)}) copy-start(bf16[8,128,1024]{2,1,0:T(8,128)(2,1)} %copy.12) | copy-start | bytes 6291460
  103.6 125.5 %all-gather.5.cloned.1.call-start = ((), (), s32[]{:S(2)}) async-start(), calls=%async_computation.4 | async-start | bytes 4718592 | tf_op jit(solution)/shard_map/all_gather | solution.py:35
Sparse Core Ops, SparseCore 0:
  10.1 48.6 all-gather.2
  103.7 68.1 reduce-scatter.1
  195.1 33.9 all-gather.4
where the time goes:
time: 307 us; the launch traced here: 306 us
  waiting for transfers between devices  150 us (49%)
  blocking collectives  81.5 us (27%)
  matrix products  22 us (7%)
  other arithmetic  20.6 us (7%)
  between operations  17.3 us (6%)
  local copies, waits for them, and re-layouts  14.3 us (5%)
    reduce_scatter x1, waiting for transfers between devices, local(): rotated = lax.psum_scatter(partial, 'dp', scatter_dimension=0, tiled=True)  67.6 us
    all_gather x1, waiting for transfers between devices, local(): features = lax.all_gather(hidden, 'tensor', axis=1, tiled=True)  49.5 us
    psum x1, blocking collectives, local(): grad_square = lax.psum(jnp.sum(gradient * gradient), ('dp', 'tensor'))  39.6 us
    all_gather x1, waiting for transfers between devices, local(): lax.all_gather(error_slope, 'dp', axis=0, tiled=True)  32.9 us
    all_to_all x1, blocking collectives, local(): lax.all_to_all(features, 'dp', split_axis=1, concat_axis=0, tiled=True)  30.2 us
    dot_general x1, matrix products, local(): jnp.dot(column_blocks, narrow_rotation, preferred_element_type=jnp.float32)  11.9 us
    unnamed x8, local copies, waits for them, and re-layouts  11.7 us
    psum x1, blocking collectives, local(): token_square = lax.psum(jnp.sum(scaled * scaled, axis=1), 'tensor')  11.7 us
  transfers between devices with their start and end apart: 3, of which 3 were waited for; matrix products, arithmetic and copies ran while one was open for 0% of the time, Pallas kernels for 0%

commit v1 on v0

--- a/solution.py
+++ b/solution.py
@@ -8,9 +8,22 @@
 SEQ = 64
 
 
+def collect(x, axis, dim):
+    ways = lax.axis_size(axis)
+    up = [(d, (d + 1) % ways) for d in range(ways)]
+    down = [(d, (d - 1) % ways) for d in range(ways)]
+    earlier, later = ([x], [x])
+    for _ in range(ways // 2):
+        earlier.append(lax.ppermute(earlier[-1], axis, up))
+    for _ in range((ways - 1) // 2):
+        later.append(lax.ppermute(later[-1], axis, down))
+    line = jnp.concatenate([*earlier[::-1], *later[1:]], axis=dim)
+    return jnp.roll(line, (lax.axis_index(axis) - ways // 2) * x.shape[dim], axis=dim)
+
+
 def local(hidden, rotation, channel_scale, lengths):
     narrow_rotation = rotation.astype(jnp.bfloat16)
-    features = lax.all_gather(hidden, "tensor", axis=1, tiled=True)
+    features = collect(hidden, "tensor", 1)
     column_blocks = lax.all_to_all(features, "dp", split_axis=1, concat_axis=0, tiled=True)
     partial = jnp.dot(column_blocks, narrow_rotation, preferred_element_type=jnp.float32)
     rotated = lax.psum_scatter(partial, "dp", scatter_dimension=0, tiled=True)

time: 307 us -> 290 us (0.945)
  waiting for transfers between devices: 150 us -> 136 us
  local copies, waits for them, and re-layouts: 14.3 us -> 5.15 us
  starting transfers between devices: 0.12 us -> 6.98 us
    all_gather x1 -> x0, waiting for transfers between devices: 49.5 us -> none  [local(): features = lax.all_gather(hidden, 'tensor', axis=1, tiled=True)]
    ppermute x0 -> x3, waiting for transfers between devices: none -> 34.3 us  [the longest x2 26.8 us: collect(): earlier.append(lax.ppermute(earlier[-1], axis, up))]
    unnamed x8 -> x14, local copies, waits for them, and re-layouts: 11.7 us -> 2.34 us
    ppermute x0 -> x3, starting transfers between devices: none -> 6.9 us  [the longest x1 3.82 us: collect(): later.append(lax.ppermute(later[-1], axis, down))]
  transfers between devices with their start and end apart: 3 -> 5, of which waited for: 3 -> 5; matrix products, arithmetic and copies ran while one was open for 0% -> 0% of each run, Pallas kernels for 0% -> 0%
where the time goes in v1:
time: 290 us
  waiting for transfers between devices  136 us (47%)
  blocking collectives  81.1 us (28%)
  matrix products  22.1 us (8%)
  other arithmetic  20.5 us (7%)
  between operations  17.8 us (6%)
  starting transfers between devices  6.98 us (2%)
  local copies, waits for them, and re-layouts  5.15 us (2%)
    reduce_scatter x1, waiting for transfers between devices, local(): rotated = lax.psum_scatter(partial, 'dp', scatter_dimension=0, tiled=True)  68.9 us
    psum x1, blocking collectives, local(): grad_square = lax.psum(jnp.sum(gradient * gradient), ('dp', 'tensor'))  39.6 us
    all_gather x1, waiting for transfers between devices, local(): lax.all_gather(error_slope, 'dp', axis=0, tiled=True)  32.9 us
    all_to_all x1, blocking collectives, local(): lax.all_to_all(features, 'dp', split_axis=1, concat_axis=0, tiled=True)  29.9 us
    ppermute x2, waiting for transfers between devices, collect(): earlier.append(lax.ppermute(earlier[-1], axis, up))  26.8 us
    dot_general x1, matrix products, local(): jnp.dot(column_blocks, narrow_rotation, preferred_element_type=jnp.float32)  11.9 us
    psum x1, blocking collectives, local(): token_square = lax.psum(jnp.sum(scaled * scaled, axis=1), 'tensor')  11.7 us
    dot_general x1, matrix products, local(): lax.dot_general(column_blocks, lax.all_gather(error_slope, 'dp', axis=0,...  10.2 us
  transfers between devices with their start and end apart: 5, of which 5 were waited for; matrix products, arithmetic and copies ran while one was open for 0% of the time, Pallas kernels for 0%

profile of v1, /device:TPU:0, one launch (start us, length us, event | category | flops | bytes accessed | tf_op | source)
XLA Modules:
  0.0 289.7 jit_solution(11695082299080600296)
XLA Ops:
  7.2 0.0 reduce-scatter.2.cloned.1.call-start
  7.2 1.3 copy.11
  8.5 3.1 %collective-permute-start = (bf16[128,2048]{0,1:T(8,128)(2,1)S(1)}, bf16[128,2048]{0,1:T(8,128)(2,1)S(1)}, u32[]{:S(2)}, u32[]{:S(2)}) collective-permute-start(bf16[128,2048]{0,1:T(8,128)(2,1)S(1)} %copy.11), channel_id=1, source_target_pairs={{0,1},{1,2},{2,3},{3,0},{4,5},{5,6},{6,7},{7,4},{8,9},{9,10},{10,1... | collective-permute-start | bytes 1572872 | tf_op jit(solution)/shard_map/ppermute | solution.py:17
  11.6 13.9 %collective-permute-done = bf16[128,2048]{0,1:T(8,128)(2,1)S(1)} collective-permute-done((bf16[128,2048]{0,1:T(8,128)(2,1)S(1)}, bf16[128,2048]{0,1:T(8,128)(2,1)S(1)}, u32[]{:S(2)}, u32[]{:S(2)}) %collective-permute-start) | collective-permute-done | bytes 524320 | tf_op jit(solution)/shard_map/ppermute | solution.py:17
  25.6 0.0 collective-permute-start.1
  25.6 3.8 %collective-permute-start.2 = (bf16[128,2048]{0,1:T(8,128)(2,1)S(1)}, bf16[128,2048]{0,1:T(8,128)(2,1)S(1)}, u32[]{:S(2)}, u32[]{:S(2)}) collective-permute-start(bf16[128,2048]{0,1:T(8,128)(2,1)S(1)} %copy.11), channel_id=1, source_target_pairs={{0,3},{1,0},{2,1},{3,2},{4,7},{5,4},{6,5},{7,6},{8,11},{9,8},{10,9... | collective-permute-start | bytes 1572872 | tf_op jit(solution)/shard_map/ppermute | solution.py:19
  29.4 12.8 %collective-permute-done.1 = bf16[128,2048]{0,1:T(8,128)(2,1)S(1)} collective-permute-done((bf16[128,2048]{0,1:T(8,128)(2,1)S(1)}, bf16[128,2048]{0,1:T(8,128)(2,1)S(1)}, u32[]{:S(2)}, u32[]{:S(2)}) %collective-permute-start.1) | collective-permute-done | bytes 524320 | tf_op jit(solution)/shard_map/ppermute | solution.py:17
  42.3 0.1 constant_dynamic-update-slice_fusion.6
  42.3 0.1 constant_dynamic-update-slice_fusion.5
  42.4 7.5 %collective-permute-done.2 = bf16[128,2048]{0,1:T(8,128)(2,1)S(1)} collective-permute-done((bf16[128,2048]{0,1:T(8,128)(2,1)S(1)}, bf16[128,2048]{0,1:T(8,128)(2,1)S(1)}, u32[]{:S(2)}, u32[]{:S(2)}) %collective-permute-start.2) | collective-permute-done | bytes 524320 | tf_op jit(solution)/shard_map/ppermute | solution.py:19
  49.9 0.1 constant_dynamic-update-slice_fusion.4
  50.0 0.1 constant_dynamic-update-slice_fusion.3
  50.0 0.1 constant_dynamic-update-slice_fusion.2
  50.1 0.1 constant_dynamic-update-slice_fusion.1
  50.2 0.1 constant_dynamic-update-slice_fusion
  50.3 0.1 constant_dynamic-slice_fusion
  50.4 29.9 %all_to_all.19 = bf16[128,8,1024]{0,2,1:T(8,128)(2,1)S(1)} all-to-all(bf16[128,8,1024]{0,2,1:T(8,128)(2,1)S(1)} %bitcast.6), channel_id=1, replica_groups=mesh['dp'=8,'tensor'=4] {'dp'}, dimensions={1} | all-to-all | bytes 4194304 | tf_op jit(solution)/shard_map/all_to_all | solution.py:27
  80.3 2.6 copy.15
  82.9 11.9 %fusion = f32[1024,2048]{1,0:T(8,128)} fusion(bf16[1024,1024]{1,0:T(8,128)(2,1)} %bitcast.8, f32[1024,2048]{1,0:T(8,128)} %param.5), kind=kOutput, calls=%fused_computation.2 | convolution fusion | flops 4297064448 | bytes 18874368 | tf_op jit(solution)/shard_map/dot_general | solution.py:28
  94.8 0.0 copy-start.2
  94.8 0.0 copy-start.1
  94.8 0.0 copy-start
  94.8 0.0 reduce-scatter.2.cloned.1.call-update
  94.9 0.0 all-gather.2.cloned.1.call-start
  94.9 0.6 copy-done.2
  95.5 0.1 fusion.2
  95.6 68.9 %reduce-scatter.2.cloned.1.call-done = f32[128,2048]{1,0:T(8,128)} async-done(((f32[1024,2048]{1,0:T(8,128)}), f32[128,2048]{1,0:T(8,128)}) %reduce-scatter.2.cloned.1.call-update) | async-done | bytes 1048592 | tf_op jit(solution)/shard_map/reduce_scatter | solution.py:29
  164.5 0.0 copy-done.1
  164.5 1.4 multiply_reduce_fusion.2
  165.9 11.7 %psum.28 = f32[128]{0:T(128)S(1)} all-reduce(f32[128]{0:T(128)S(1)} %multiply_reduce_fusion.2), channel_id=1, replica_groups=mesh['dp'=8,'tensor'=4] {'tensor'}, use_global_device_ids=true, to_apply=%region_3.4 | all-reduce | flops 128 | bytes 1024 | tf_op jit(solution)/shard_map/psum | solution.py:31
  177.6 9.9 %multiply_reduce_fusion.1 = (f32[]{:T(128)}, bf16[128,2048]{1,0:T(8,128)(2,1)}) fusion(f32[128]{0:T(128)S(1)} %fusion.2, f32[128]{0:T(128)S(1)} %get-tuple-element.7, f32[128,2048]{1,0:T(8,128)} %reduce-scatter.2.cloned.1.call-done, f32[2048]{0:T(1024)S(1)} %copy-done.1, f32[128]{0:T(128)S(1)} %get-tuple-element.8), kind=kLoop, calls=%fused_computation.4 | loop fusion | flops 2621439 | bytes 1582596 | tf_op jit(solution)/shard_map/reduce_sum | solution.py:41
  187.5 0.0 all-gather.2.cloned.1.call-update
  187.5 0.6 reduce_sum.49
  188.7 32.9 %all-gather.2.cloned.1.call-done = bf16[1024,2048]{1,0:T(8,128)(2,1)} async-done(((bf16[128,2048]{1,0:T(8,128)(2,1)}), bf16[1024,2048]{1,0:T(8,128)(2,1)}) %all-gather.2.cloned.1.call-update) | async-done | bytes 4194320 | tf_op jit(solution)/shard_map/all_gather | solution.py:48
  221.6 0.0 copy-done
  221.6 10.2 %multiply_reduce_fusion = (f32[]{:T(128)}, f32[1024,2048]{1,0:T(8,128)}) fusion(bf16[1024,1024]{1,0:T(8,128)(2,1)S(1)} %bitcast.9, bf16[1024,2048]{1,0:T(8,128)(2,1)} %all-gather.2.cloned.1.call-done), kind=kOutput, calls=%fused_computation | convolution fusion | flops 4299161600 | bytes 14680068 | tf_op jit(solution)/shard_map/dot_general | solution.py:46
  231.8 39.6 %all-reduce = (f32[]{:T(128)}, f32[]{:T(128)}, f32[]{:T(128)}) all-reduce(f32[]{:T(128)} %get-tuple-element.9, f32[]{:T(128)} %get-tuple-element.5, f32[]{:T(128)S(6)} %div.55), channel_id=1, replica_groups=mesh['dp'=8,'tensor'=4] {'dp','tensor'}, use_global_device_ids=true, to_apply=%region_5.6 | all-reduce | flops 3 | bytes 24 | tf_op jit(solution)/shard_map/psum | solution.py:53
  273.3 8.4 %broadcast_divide_fusion = f32[1024,2048]{1,0:T(8,128)} fusion(f32[1024,2048]{1,0:T(8,128)} %get-tuple-element.10, f32[]{:T(128)S(6)} %sqrt.7), kind=kLoop, calls=%fused_computation.1 | loop fusion | flops 2097152 | bytes 16777220 | tf_op jit(solution)/shard_map/div | solution.py:54
  (3 shorter events, 0.1 us)
Async XLA Ops:
  7.2 157.3 %reduce-scatter.2.cloned.1.call-start = ((), (), s32[]{:S(2)}) async-start(), calls=%async_computation.2 | async-start | bytes 9437184 | tf_op jit(solution)/shard_map/reduce_scatter | solution.py:29
  8.5 17.0 %collective-permute-start = (bf16[128,2048]{0,1:T(8,128)(2,1)S(1)}, bf16[128,2048]{0,1:T(8,128)(2,1)S(1)}, u32[]{:S(2)}, u32[]{:S(2)}) collective-permute-start(bf16[128,2048]{0,1:T(8,128)(2,1)S(1)} %copy.11), channel_id=1, source_target_pairs={{0,1},{1,2},{2,3},{3,0},{4,5},{5,6},{6,7},{7,4},{8,9},{9,10},{10,1... | collective-permute-start | bytes 1572872 | tf_op jit(solution)/shard_map/ppermute | solution.py:17
  25.6 16.7 %collective-permute-start.1 = (bf16[128,2048]{0,1:T(8,128)(2,1)S(1)}, bf16[128,2048]{0,1:T(8,128)(2,1)S(1)}, u32[]{:S(2)}, u32[]{:S(2)}) collective-permute-start(bf16[128,2048]{0,1:T(8,128)(2,1)S(1)} %collective-permute-done), channel_id=1, source_target_pairs={{0,1},{1,2},{2,3},{3,0},{4,5},{5,6},{6,7},{7,4},{8,9},{9,10},{10,1... | collective-permute-start | bytes 1572872 | tf_op jit(solution)/shard_map/ppermute | solution.py:17
  25.6 24.3 %collective-permute-start.2 = (bf16[128,2048]{0,1:T(8,128)(2,1)S(1)}, bf16[128,2048]{0,1:T(8,128)(2,1)S(1)}, u32[]{:S(2)}, u32[]{:S(2)}) collective-permute-start(bf16[128,2048]{0,1:T(8,128)(2,1)S(1)} %copy.11), channel_id=1, source_target_pairs={{0,3},{1,0},{2,1},{3,2},{4,7},{5,4},{6,5},{7,6},{8,11},{9,8},{10,9... | collective-permute-start | bytes 1572872 | tf_op jit(solution)/shard_map/ppermute | solution.py:19
  94.8 0.7 copy-start.2
  94.8 69.6 %copy-start.1 = (f32[2048]{0:T(1024)S(1)}, f32[2048]{0:T(1024)}, u32[]{:S(2)}) copy-start(f32[2048]{0:T(1024)} %param.6) | copy-start | bytes 24580
  94.8 126.8 %copy-start = (bf16[8,128,1024]{2,1,0:T(8,128)(2,1)S(1)}, bf16[8,128,1024]{2,1,0:T(8,128)(2,1)}, u32[]{:S(2)}) copy-start(bf16[8,128,1024]{2,1,0:T(8,128)(2,1)} %copy.15) | copy-start | bytes 6291460
  94.9 126.7 %all-gather.2.cloned.1.call-start = ((), (), s32[]{:S(2)}) async-start(), calls=%async_computation.3 | async-start | bytes 4718592 | tf_op jit(solution)/shard_map/all_gather | solution.py:48
Sparse Core Ops, SparseCore 0:
  95.0 69.4 reduce-scatter.1
  187.6 33.9 all-gather.1
